TPU v7x, 32 devices: a whole 2x2x4 slice. The times are simulated.
32 devices in a mesh: vel: 8 (over z, y), space: 4 (over x, core).
Axes of the slice: x: 2, y: 2, z: 4, core: 2. Of those that a mesh axis runs over, the one named last changes fastest.
Arguments:
- initial: float32 [13824, 16, 128], P('vel', 'space'), as said below
- site_kind: int32 [16, 128], P('space'), may hold values from 0 to 2, as said below
Outputs:
- distribution: float32 [13824, 16, 128], P('vel', 'space')
- kelvin_level: float32 [16, 128], P('space')
Inputs may be any that keep to these rules, and one draw needn't show every extreme that they name: `site_kind`: 0 marks a gas cell, 1 a wall cell, 2 an inflow cell. `initial`: every entry is positive.
All inputs are finite; a program needn't handle non-finite values.
Results may differ from a plain program's by a relative error of at most 0.0003.
Values sent between devices are 32-bit elements; how exact they have to be, the bound alone decides.
A program may use at most 64 MiB of HBM per device.

v0:
```python
import math

import jax
import jax.numpy as jnp
from jax import lax
from jax.sharding import PartitionSpec as P

NVX = 24
STEPS = 2


speed_limit = 4.0
courant = 0.1
diffusivity_ratio = 2.0 / 3.0
power_law_index = 0.81
encounter_rate = 0.25
wall_kelvin = 1.0
inflow_concentration = 1.0
inflow_speed = 0.5
inflow_kelvin = 1.0


def with_halo(block, sides, width):
    for axis, dim in sides:
        count = lax.axis_size(axis)
        forward = [(i, i + 1) for i in range(count - 1)]
        backward = [(target, source) for source, target in forward]
        low = lax.ppermute(
            lax.slice_in_dim(block, block.shape[dim] - width, None, axis=dim), axis, forward
        )
        high = lax.ppermute(lax.slice_in_dim(block, 0, width, axis=dim), axis, backward)
        block = jnp.concatenate([low, block, high], axis=dim)
    return block


def speeds(offset, amount):
    index = offset + jnp.arange(amount, dtype=jnp.int32)
    spacing = 2.0 * speed_limit / (NVX - 1)
    along_x_part = -speed_limit + spacing * (index // (NVX * NVX)).astype(jnp.float32)
    along_y_part = -speed_limit + spacing * (index // NVX % NVX).astype(jnp.float32)
    along_z_part = -speed_limit + spacing * (index % NVX).astype(jnp.float32)
    return (along_x_part, along_y_part, along_z_part)


def quad_weight():
    return (2.0 * speed_limit / (NVX - 1)) ** 3 / (2.0 * math.pi) ** 1.5


def minmod(left, right):
    return 0.5 * (jnp.sign(left) + jnp.sign(right)) * jnp.minimum(jnp.abs(left), jnp.abs(right))


def sweep(distribution_table, number, along):
    length = distribution_table.shape[along]

    def piece(source, low, high):
        return lax.slice_in_dim(source, low, high, axis=along)

    jumps = piece(distribution_table, 1, length) - piece(distribution_table, 0, length - 1)
    slopes = minmod(piece(jumps, 0, length - 2), piece(jumps, 1, length - 1))
    left_face = piece(distribution_table, 1, length - 2) + 0.5 * (1.0 - number) * piece(
        slopes, 0, length - 3
    )
    right_face = piece(distribution_table, 2, length - 1) - 0.5 * (1.0 + number) * piece(
        slopes, 1, length - 2
    )
    flux = number * jnp.where(number > 0, left_face, right_face)
    return piece(distribution_table, 2, length - 2) - (
        piece(flux, 1, length - 3) - piece(flux, 0, length - 4)
    )


def transport(padded, along_x_part, along_y_part):
    swept = sweep(padded, courant * along_x_part[:, None, None], 1)
    widened = jnp.pad(swept, ((0, 0), (0, 0), (2, 2)))
    return sweep(widened, courant * along_y_part[:, None, None], 2)


def macroscopic_moments(advected_distribution, along_x_part, along_y_part, along_z_part):
    magnitude_squares = (
        along_x_part * along_x_part + along_y_part * along_y_part + along_z_part * along_z_part
    )
    ones = jnp.ones_like(along_x_part)
    table = quad_weight() * jnp.stack(
        [ones, along_x_part, along_y_part, along_z_part, magnitude_squares]
    )
    local = jnp.einsum("kv,vrc->krc", table, advected_distribution, precision=lax.Precision.HIGHEST)
    integral_totals = lax.psum(local, "vel")
    particle_concentration = integral_totals[0]
    average_drift_x = integral_totals[1] / particle_concentration
    average_drift_y = integral_totals[2] / particle_concentration
    average_drift_z = integral_totals[3] / particle_concentration
    kelvin_level = (
        integral_totals[4] / particle_concentration
        - (
            average_drift_x * average_drift_x
            + average_drift_y * average_drift_y
            + average_drift_z * average_drift_z
        )
    ) / 3.0
    rel_x = along_x_part[:, None, None] - average_drift_x[None]
    rel_y = along_y_part[:, None, None] - average_drift_y[None]
    rel_z = along_z_part[:, None, None] - average_drift_z[None]
    scaled = (
        0.5
        * quad_weight()
        * (rel_x * rel_x + rel_y * rel_y + rel_z * rel_z)
        * advected_distribution
    )
    local_heat = jnp.stack(
        [
            jnp.sum(rel_x * scaled, axis=0),
            jnp.sum(rel_y * scaled, axis=0),
            jnp.sum(rel_z * scaled, axis=0),
        ]
    )
    conductive_transfer = lax.psum(local_heat, "vel")
    return (
        particle_concentration,
        average_drift_x,
        average_drift_y,
        average_drift_z,
        kelvin_level,
        conductive_transfer,
    )


def approach_increment(
    advected_distribution, kind_labels, along_x_part, along_y_part, along_z_part
):
    (
        particle_concentration,
        average_drift_x,
        average_drift_y,
        average_drift_z,
        kelvin_level,
        conductive_transfer,
    ) = macroscopic_moments(advected_distribution, along_x_part, along_y_part, along_z_part)
    rel_x = along_x_part[:, None, None] - average_drift_x[None]
    rel_y = along_y_part[:, None, None] - average_drift_y[None]
    rel_z = along_z_part[:, None, None] - average_drift_z[None]
    relative_magnitude_square = rel_x * rel_x + rel_y * rel_y + rel_z * rel_z
    stress_scalar_grid = particle_concentration * kelvin_level
    gaussian_local_balance = (
        particle_concentration
        * kelvin_level ** (-1.5)
        * jnp.exp(-relative_magnitude_square / (2.0 * kelvin_level))
    )
    conductive_vector_slot = (
        rel_x * conductive_transfer[0]
        + rel_y * conductive_transfer[1]
        + rel_z * conductive_transfer[2]
    )
    corrected_goal_distribution = gaussian_local_balance * (
        1.0
        + (1.0 - diffusivity_ratio)
        * conductive_vector_slot
        * (relative_magnitude_square / kelvin_level - 5.0)
        / (5.0 * stress_scalar_grid * kelvin_level)
    )
    approach_rate = (
        encounter_rate * particle_concentration * kelvin_level ** (1.0 - power_law_index)
    )
    relaxed = advected_distribution + approach_rate * (
        corrected_goal_distribution - advected_distribution
    )
    magnitude_squares = (
        along_x_part * along_x_part + along_y_part * along_y_part + along_z_part * along_z_part
    )[:, None, None]
    wall_distribution = (
        particle_concentration
        * wall_kelvin ** (-1.5)
        * jnp.exp(-magnitude_squares / (2.0 * wall_kelvin))
    )
    inflow_magnitude_square = (
        (along_x_part - inflow_speed) ** 2
        + along_y_part * along_y_part
        + along_z_part * along_z_part
    )[:, None, None]
    inflow_distribution = (
        inflow_concentration
        * inflow_kelvin ** (-1.5)
        * jnp.exp(-inflow_magnitude_square / (2.0 * inflow_kelvin))
    )
    revised_distribution = jnp.where(
        kind_labels == 1,
        wall_distribution,
        jnp.where(kind_labels == 2, inflow_distribution, relaxed),
    )
    return (revised_distribution, kelvin_level)


def per_device(initial, site_kind):
    amount = initial.shape[0]
    along_x_part, along_y_part, along_z_part = speeds(lax.axis_index("vel") * amount, amount)
    distribution_table = initial
    kelvin_level = jnp.zeros(site_kind.shape, jnp.float32)
    for section in range(STEPS):
        padded = with_halo(distribution_table, (("space", 1),), 2)
        advected_distribution = transport(padded, along_x_part, along_y_part)
        distribution_table, kelvin_level = approach_increment(
            advected_distribution, site_kind, along_x_part, along_y_part, along_z_part
        )
    return (distribution_table, kelvin_level)


def solution(mesh):
    return jax.shard_map(
        per_device,
        mesh=mesh,
        in_specs=(P("vel", "space", None), P("space", None)),
        out_specs=(P("vel", "space", None), P("space", None)),
        check_vma=False,
    )
```

profile of v0, /device:TPU:6, one launch (start us, length us, event | category | flops | bytes accessed | tf_op | source)
XLA Modules:
  0.0 278.4 jit_solution(12052999114648105756)
XLA Ops:
  8.0 3.6 %collective-permute-start.1 = (f32[1728,2,128]{2,0,1:T(8,128)}, f32[1728,2,128]{2,0,1:T(8,128)}, u32[]{:S(2)}, u32[]{:S(2)}) collective-permute-start(f32[1728,2,128]{2,0,1:T(8,128)} %get-tuple-element.21), channel_id=1, source_target_pairs={{1,0},{2,1},{3,2},{5,4},{6,5},{7,6},{9,8},{10,9},{11,10},{13,12},{... | collective-permute-start | bytes 5308424 | tf_op jit(solution)/shard_map/ppermute | solution.py:31
  18.4 11.8 %collective-permute-done = f32[1728,2,128]{2,0,1:T(8,128)} collective-permute-done((f32[1728,2,128]{2,0,1:T(8,128)}, f32[1728,2,128]{2,0,1:T(8,128)}, u32[]{:S(2)}, u32[]{:S(2)}) %collective-permute-start) | collective-permute-done | bytes 1769504 | tf_op jit(solution)/shard_map/ppermute | solution.py:28
  36.4 3.7 %fusion.16 = f32[1728,5,128]{2,0,1:T(8,128)S(1)} fusion(f32[1728,6,128]{2,0,1:T(8,128)S(1)} %minimum_multiply_fusion.3, f32[1728,2,128]{2,0,1:T(8,128)} %collective-permute-done.1, f32[1728,4,128]{2,0,1:T(8,128)S(1)} %copy-done.2, f32[1728,2,128]{2,0,1:T(8,128)} %collective-permute-done, f32[1728]{0:T(1024)S(1)} %get-tuple-element.53, ...), kind=kLoop, calls=%fused_computation.58 | loop fusion | flops 8847360 | bytes 20371392 | tf_op jit(solution)/shard_map/mul | solution.py:67
  40.6 3.7 %fusion.3 = f32[1728,4,131]{2,0,1:T(8,128)S(1)} fusion(f32[1728,4,128]{2,0,1:T(8,128)S(1)} %fusion.71), kind=kLoop, calls=%fused_computation.11 | loop fusion | flops 905472 | bytes 7160832 | tf_op jit(solution)/shard_map/sub | solution.py:59
  44.3 4.9 %minimum_multiply_fusion.1 = f32[1728,4,130]{2,0,1:T(8,128)S(1)} fusion(f32[1728,4,131]{2,0,1:T(8,128)S(1)} %fusion.3), kind=kLoop, calls=%fused_computation.24 | loop fusion | flops 7188480 | bytes 10782720 | tf_op jit(solution)/shard_map/mul | solution.py:50
  49.2 5.3 %fusion.2 = f32[1728,4,129]{2,0,1:T(8,128)S(1)} fusion(f32[1728,4,128]{2,0,1:T(8,128)S(1)} %fusion.71, f32[1728,4,130]{2,0,1:T(8,128)S(1)} %minimum_multiply_fusion.1, f32[1728]{0:T(1024)S(1)} %get-tuple-element.51, f32[1728]{0:T(1024)S(1)} %get-tuple-element.52, f32[1728]{0:T(1024)S(1)} %get-tuple-element.61, pred[1728]{0:T(1024)(128)(4,1)S(1)} %copy-done.39), kind=kLoop, calls=%fused_computation.10 | loop fusion | flops 5349888 | bytes 14261184 | tf_op jit(solution)/shard_map/mul | solution.py:67
  55.5 2.4 fusion.74
  57.9 32.9 %psum.28 = f32[5,4,128]{2,0,1:T(8,128)} all-reduce(f32[5,4,128]{2,0,1:T(8,128)} %fusion.74), channel_id=1, replica_groups=mesh['vel'=8,'space'=4] {'vel'}, use_global_device_ids=true, to_apply=%region_0.1 | all-reduce | flops 2560 | bytes 20480 | tf_op jit(solution)/shard_map/psum | solution.py:88
  93.7 3.0 %fusion.20 = (f32[4,128]{1,0:T(4,128)S(1)}, f32[4,128]{1,0:T(4,128)S(1)}, f32[4,128]{1,0:T(4,128)S(1)}) fusion(f32[4,128]{1,0:T(4,128)S(1)} %bitcast.90, f32[1728]{0:T(1024)S(1)} %broadcast_add_fusion, f32[4,128]{1,0:T(4,128)S(1)} %bitcast.96, f32[1728]{0:T(1024)} %get-tuple-element.48, f32[4,128]{1,0:T(4,128)S(1)} %bitcast.93, ...), kind=kLoop, calls=%fused_computation.65 | loop fusion | flops 14154240 | bytes 3571968 | tf_op jit(solution)/shard_map/reduce_sum | solution.py:112
  97.3 23.8 %psum.29 = f32[3,4,128]{2,1,0:T(4,128)} all-reduce(f32[3,4,128]{2,1,0:T(4,128)} %pad_maximum_fusion.5), channel_id=1, replica_groups=mesh['vel'=8,'space'=4] {'vel'}, use_global_device_ids=true, to_apply=%region_4.5 | all-reduce | flops 1536 | bytes 12288 | tf_op jit(solution)/shard_map/psum | solution.py:117
  121.8 9.9 %fusion.42 = f32[1728,4,128]{2,0,1:T(8,128)S(1)} fusion(f32[1728,4,128]{2,0,1:T(8,128)S(1)} %fusion.70, f32[4,128]{1,0:T(4,128)} %bitcast.105, f32[4,128]{1,0:T(4,128)} %bitcast.111, f32[4,128]{1,0:T(4,128)S(1)} %get-tuple-element.37, f32[4,128]{1,0:T(4,128)S(1)} %get-tuple-element.38, f32[4,128]{1,0:T(4,128)S(1)} %get-tuple-element.36, ...), kind=kLoop, calls=%fused_computation.87 | loop fusion | flops 25657344 | bytes 7138048 | tf_op jit(solution)/shard_map/jit(_where)/select_n | solution.py:185
  133.9 3.6 %collective-permute-start.3 = (f32[1728,2,128]{2,0,1:T(8,128)S(1)}, f32[1728,2,128]{2,0,1:T(8,128)S(1)}, u32[]{:S(2)}, u32[]{:S(2)}) collective-permute-start(f32[1728,2,128]{2,0,1:T(8,128)S(1)} %get-tuple-element.20), channel_id=1, source_target_pairs={{1,0},{2,1},{3,2},{5,4},{6,5},{7,6},{9,8},{10,9},{11,10},{13,12},{... | collective-permute-start | bytes 5308424 | tf_op jit(solution)/shard_map/ppermute | solution.py:31
  137.5 18.3 %collective-permute-done.2 = f32[1728,2,128]{2,0,1:T(8,128)S(1)} collective-permute-done((f32[1728,2,128]{2,0,1:T(8,128)S(1)}, f32[1728,2,128]{2,0,1:T(8,128)S(1)}, u32[]{:S(2)}, u32[]{:S(2)}) %collective-permute-start.2) | collective-permute-done | bytes 1769504 | tf_op jit(solution)/shard_map/ppermute | solution.py:28
  158.8 3.0 %slice_subtract_fusion = f32[1728,7,128]{2,0,1:T(8,128)} fusion(f32[1728,8,128]{2,0,1:T(8,128)S(1)} %pad_maximum_fusion), kind=kLoop, calls=%fused_computation.43 | loop fusion | flops 1548288 | bytes 18579456 | tf_op jit(solution)/shard_map/sub | solution.py:59
  161.8 7.6 %minimum_multiply_fusion.2 = f32[1728,6,128]{2,0,1:T(8,128)S(1)} fusion(f32[1728,7,128]{2,0,1:T(8,128)} %slice_subtract_fusion), kind=kLoop, calls=%fused_computation.45 | loop fusion | flops 10616832 | bytes 15925248 | tf_op jit(solution)/shard_map/mul | solution.py:50
  171.8 9.0 %fusion.69 = f32[1728,4,128]{2,0,1:T(8,128)S(1)} fusion(f32[1728,5,128]{2,0,1:T(8,128)S(1)} %fusion.12, f32[1728,4,128]{2,0,1:T(8,128)S(1)} %fusion.70, f32[4,128]{1,0:T(4,128)S(1)} %bitcast.106, f32[4,128]{1,0:T(4,128)S(1)} %bitcast.112, f32[4,128]{1,0:T(4,128)S(1)} %get-tuple-element.37, f32[4,128]{1,0:T(4,128)S(1)} %get-tuple-element.38, ...), kind=kLoop, calls=%fused_computation.116 | loop fusion | flops 27426816 | bytes 14215936 | tf_op jit(solution)/shard_map/sub | solution.py:68
  180.8 3.7 %fusion.8 = f32[1728,4,131]{2,0,1:T(8,128)S(1)} fusion(f32[1728,4,128]{2,0,1:T(8,128)S(1)} %fusion.69), kind=kLoop, calls=%fused_computation.16 | loop fusion | flops 905472 | bytes 7160832 | tf_op jit(solution)/shard_map/sub | solution.py:59
  184.5 5.3 %minimum_multiply_fusion = f32[1728,4,130]{2,0,1:T(8,128)S(1)} fusion(f32[1728,4,131]{2,0,1:T(8,128)S(1)} %fusion.8), kind=kLoop, calls=%fused_computation.23 | loop fusion | flops 7188480 | bytes 10782720 | tf_op jit(solution)/shard_map/mul | solution.py:50
  189.8 5.3 %fusion.7 = f32[1728,4,129]{2,0,1:T(8,128)S(1)} fusion(f32[1728,4,128]{2,0,1:T(8,128)S(1)} %fusion.69, f32[1728,4,130]{2,0,1:T(8,128)S(1)} %minimum_multiply_fusion, f32[1728]{0:T(1024)S(1)} %copy-done.11, f32[1728]{0:T(1024)S(1)} %copy-done.13, f32[1728]{0:T(1024)S(1)} %copy-done.15, pred[1728]{0:T(1024)(128)(4,1)S(1)} %copy-done.40), kind=kLoop, calls=%fused_computation.15 | loop fusion | flops 5349888 | bytes 14261184 | tf_op jit(solution)/shard_map/mul | solution.py:67
  198.5 30.2 %psum.30 = f32[5,4,128]{2,1,0:T(4,128)} all-reduce(f32[5,4,128]{2,1,0:T(4,128)} %copy.20), channel_id=1, replica_groups=mesh['vel'=8,'space'=4] {'vel'}, use_global_device_ids=true, to_apply=%region_5.6 | all-reduce | flops 2560 | bytes 20480 | tf_op jit(solution)/shard_map/psum | solution.py:88
  232.6 2.9 %fusion.45 = (f32[4,128]{1,0:T(4,128)S(1)}, f32[4,128]{1,0:T(4,128)S(1)}, f32[4,128]{1,0:T(4,128)S(1)}) fusion(f32[4,128]{1,0:T(4,128)S(1)} %get-tuple-element.27, f32[1728]{0:T(1024)S(1)} %broadcast_add_fusion, f32[4,128]{1,0:T(4,128)S(1)} %bitcast.115, f32[1728]{0:T(1024)} %get-tuple-element.48, f32[4,128]{1,0:T(4,128)S(1)} %bitcast.113, ...), kind=kLoop, calls=%fused_computation.90 | loop fusion | flops 14154240 | bytes 3571968 | tf_op jit(solution)/shard_map/reduce_sum | solution.py:112
  236.2 22.8 %psum.31 = f32[3,4,128]{2,1,0:T(4,128)} all-reduce(f32[3,4,128]{2,1,0:T(4,128)} %pad_maximum_fusion.6), channel_id=1, replica_groups=mesh['vel'=8,'space'=4] {'vel'}, use_global_device_ids=true, to_apply=%region_9.10 | all-reduce | flops 1536 | bytes 12288 | tf_op jit(solution)/shard_map/psum | solution.py:117
  259.7 9.9 %fusion.67 = f32[1728,4,128]{2,0,1:T(8,128)S(1)} fusion(f32[1728,4,128]{2,0,1:T(8,128)S(1)} %fusion.68, f32[4,128]{1,0:T(4,128)} %bitcast.129, f32[4,128]{1,0:T(4,128)} %bitcast.131, f32[4,128]{1,0:T(4,128)S(1)} %get-tuple-element.34, f32[4,128]{1,0:T(4,128)S(1)} %get-tuple-element.35, f32[4,128]{1,0:T(4,128)S(1)} %get-tuple-element.33, ...), kind=kLoop, calls=%fused_computation.112 | loop fusion | flops 25657344 | bytes 7138048 | tf_op jit(solution)/shard_map/jit(_where)/select_n | solution.py:185
  269.7 8.5 %copy.28 = f32[1728,4,128]{2,1,0:T(4,128)} copy(f32[1728,4,128]{2,0,1:T(8,128)S(1)} %fusion.67) | data formatting | bytes 7077888
  (127 shorter events, 41.5 us)
Async XLA Ops:
  5.8 26.0 %copy-start = (f32[1728,4,128]{2,1,0:T(4,128)S(1)}, f32[1728,4,128]{2,1,0:T(4,128)}, u32[]{:S(2)}) copy-start(f32[1728,4,128]{2,1,0:T(4,128)} %param.2) | copy-start | bytes 10616836
  5.8 24.4 %collective-permute-start = (f32[1728,2,128]{2,0,1:T(8,128)}, f32[1728,2,128]{2,0,1:T(8,128)}, u32[]{:S(2)}, u32[]{:S(2)}) collective-permute-start(f32[1728,2,128]{2,0,1:T(8,128)} %get-tuple-element.22), channel_id=1, source_target_pairs={{0,1},{1,2},{2,3},{4,5},{5,6},{6,7},{8,9},{9,10},{10,11},{12,13},{... | collective-permute-start | bytes 5308424 | tf_op jit(solution)/shard_map/ppermute | solution.py:28
  8.0 24.1 %collective-permute-start.1 = (f32[1728,2,128]{2,0,1:T(8,128)}, f32[1728,2,128]{2,0,1:T(8,128)}, u32[]{:S(2)}, u32[]{:S(2)}) collective-permute-start(f32[1728,2,128]{2,0,1:T(8,128)} %get-tuple-element.21), channel_id=1, source_target_pairs={{1,0},{2,1},{3,2},{5,4},{6,5},{7,6},{9,8},{10,9},{11,10},{13,12},{... | collective-permute-start | bytes 5308424 | tf_op jit(solution)/shard_map/ppermute | solution.py:31
  15.7 20.7 %copy-start.16 = (f32[1728]{0:T(1024)}, f32[1728]{0:T(1024)S(1)}, u32[]{:S(2)}) copy-start(f32[1728]{0:T(1024)S(1)} %get-tuple-element.53) | copy-start | bytes 20740
  15.7 20.7 %copy-start.18 = (f32[1728]{0:T(1024)}, f32[1728]{0:T(1024)S(1)}, u32[]{:S(2)}) copy-start(f32[1728]{0:T(1024)S(1)} %get-tuple-element.54) | copy-start | bytes 20740
  15.8 33.4 %copy-start.10 = (f32[1728]{0:T(1024)}, f32[1728]{0:T(1024)S(1)}, u32[]{:S(2)}) copy-start(f32[1728]{0:T(1024)S(1)} %get-tuple-element.51) | copy-start | bytes 20740
  15.8 33.4 %copy-start.12 = (f32[1728]{0:T(1024)}, f32[1728]{0:T(1024)S(1)}, u32[]{:S(2)}) copy-start(f32[1728]{0:T(1024)S(1)} %get-tuple-element.52) | copy-start | bytes 20740
  15.8 20.6 %copy-start.20 = (f32[1728]{0:T(1024)}, f32[1728]{0:T(1024)S(1)}, u32[]{:S(2)}) copy-start(f32[1728]{0:T(1024)S(1)} %get-tuple-element.62) | copy-start | bytes 20740
  15.8 33.4 %copy-start.14 = (f32[1728]{0:T(1024)}, f32[1728]{0:T(1024)S(1)}, u32[]{:S(2)}) copy-start(f32[1728]{0:T(1024)S(1)} %get-tuple-element.61) | copy-start | bytes 20740
  44.3 4.9 %copy-start.39 = (pred[1728]{0:T(1024)(128)(4,1)S(1)}, pred[1728]{0:T(1024)(128)(4,1)}, u32[]{:S(2)}) copy-start(pred[1728]{0:T(1024)(128)(4,1)} %get-tuple-element.59) | copy-start | bytes 5188
  92.4 4.3 %copy-start.24 = (f32[1,4,128]{2,0,1:T(1,128)}, f32[1,4,128]{2,0,1:T(1,128)S(1)}, u32[]{:S(2)}) copy-start(f32[1,4,128]{2,0,1:T(1,128)S(1)} %get-tuple-element.17) | copy-start | bytes 6148
  92.4 4.3 %copy-start.26 = (f32[1,4,128]{2,0,1:T(1,128)}, f32[1,4,128]{2,0,1:T(1,128)S(1)}, u32[]{:S(2)}) copy-start(f32[1,4,128]{2,0,1:T(1,128)S(1)} %get-tuple-element.18) | copy-start | bytes 6148
  132.0 23.8 %collective-permute-start.2 = (f32[1728,2,128]{2,0,1:T(8,128)S(1)}, f32[1728,2,128]{2,0,1:T(8,128)S(1)}, u32[]{:S(2)}, u32[]{:S(2)}) collective-permute-start(f32[1728,2,128]{2,0,1:T(8,128)S(1)} %get-tuple-element.19), channel_id=1, source_target_pairs={{0,1},{1,2},{2,3},{4,5},{5,6},{6,7},{8,9},{9,10},{10,11},{12,13},{... | collective-permute-start | bytes 5308424 | tf_op jit(solution)/shard_map/ppermute | solution.py:28
  133.9 23.7 %collective-permute-start.3 = (f32[1728,2,128]{2,0,1:T(8,128)S(1)}, f32[1728,2,128]{2,0,1:T(8,128)S(1)}, u32[]{:S(2)}, u32[]{:S(2)}) collective-permute-start(f32[1728,2,128]{2,0,1:T(8,128)S(1)} %get-tuple-element.20), channel_id=1, source_target_pairs={{1,0},{2,1},{3,2},{5,4},{6,5},{7,6},{9,8},{10,9},{11,10},{13,12},{... | collective-permute-start | bytes 5308424 | tf_op jit(solution)/shard_map/ppermute | solution.py:31
  161.8 7.6 %copy-start.4 = (f32[1728,2,128]{2,0,1:T(8,128)S(1)}, f32[1728,2,128]{2,0,1:T(8,128)}, u32[]{:S(2)}) copy-start(f32[1728,2,128]{2,0,1:T(8,128)} %copy-done.3) | copy-start | bytes 5308420
  161.8 7.7 %copy-start.17 = (f32[1728]{0:T(1024)S(1)}, f32[1728]{0:T(1024)}, u32[]{:S(2)}) copy-start(f32[1728]{0:T(1024)} %copy-done.16) | copy-start | bytes 20740
  161.8 7.7 %copy-start.19 = (f32[1728]{0:T(1024)S(1)}, f32[1728]{0:T(1024)}, u32[]{:S(2)}) copy-start(f32[1728]{0:T(1024)} %copy-done.18) | copy-start | bytes 20740
  161.8 7.7 %copy-start.21 = (f32[1728]{0:T(1024)S(1)}, f32[1728]{0:T(1024)}, u32[]{:S(2)}) copy-start(f32[1728]{0:T(1024)} %copy-done.20) | copy-start | bytes 20740
  161.8 7.7 %copy-start.29 = (pred[1728]{0:T(1024)(128)(4,1)S(1)}, pred[1728]{0:T(1024)(128)(4,1)}, u32[]{:S(2)}) copy-start(pred[1728]{0:T(1024)(128)(4,1)} %get-tuple-element.60) | copy-start | bytes 5188
  184.5 5.3 %copy-start.11 = (f32[1728]{0:T(1024)S(1)}, f32[1728]{0:T(1024)}, u32[]{:S(2)}) copy-start(f32[1728]{0:T(1024)} %copy-done.10) | copy-start | bytes 20740
  184.5 5.3 %copy-start.13 = (f32[1728]{0:T(1024)S(1)}, f32[1728]{0:T(1024)}, u32[]{:S(2)}) copy-start(f32[1728]{0:T(1024)} %copy-done.12) | copy-start | bytes 20740
  184.5 5.3 %copy-start.15 = (f32[1728]{0:T(1024)S(1)}, f32[1728]{0:T(1024)}, u32[]{:S(2)}) copy-start(f32[1728]{0:T(1024)} %copy-done.14) | copy-start | bytes 20740
  184.5 5.3 %copy-start.40 = (pred[1728]{0:T(1024)(128)(4,1)S(1)}, pred[1728]{0:T(1024)(128)(4,1)}, u32[]{:S(2)}) copy-start(pred[1728]{0:T(1024)(128)(4,1)} %get-tuple-element.59) | copy-start | bytes 5188
  232.0 3.6 %copy-start.38 = (f32[1,4,128]{2,0,1:T(1,128)}, f32[1,4,128]{2,0,1:T(1,128)S(1)}, u32[]{:S(2)}) copy-start(f32[1,4,128]{2,0,1:T(1,128)S(1)} %get-tuple-element.13) | copy-start | bytes 6148
  (23 other events, 47.0 us)
where the time goes:
time: 283 us; the launch traced here: 278 us
  blocking collectives  110 us (39%)
  other arithmetic  97.4 us (34%)
  waiting for transfers between devices  31.8 us (11%)
  local copies, waits for them, and re-layouts  22.2 us (8%)
  starting transfers between devices  11.4 us (4%)
  matrix products  4.17 us (1%)
    psum x2, blocking collectives, macroscopic_moments(): integral_totals = lax.psum(local, 'vel')  63.1 us
    psum x2, blocking collectives, macroscopic_moments(): conductive_transfer = lax.psum(local_heat, 'vel')  46.6 us
    ppermute x2, waiting for transfers between devices, with_halo(): lax.ppermute(lax.slice_in_dim(block, block.shape[dim] - width, None, axis...  30.1 us
    mul x4, other arithmetic, minmod(): 0.5 * (jnp.sign(left) + jnp.sign(right))  20 us
    select_n x2, other arithmetic, approach_increment(): jnp.where(kind_labels == 1, wall_distribution, jnp.where(kind_labels == 2...  19.8 us
    mul x4, other arithmetic, sweep(): flux = number * jnp.where(number > 0, left_face, right_face)  16.3 us
    unnamed x90, local copies, waits for them, and re-layouts  14.2 us
    sub x4, other arithmetic, sweep(): piece(distribution_table, 2, length - 2)  11.4 us
  transfers between devices with their start and end apart: 4, of which 3 were waited for; matrix products, arithmetic and copies ran while one was open for 3% of the time, Pallas kernels for 0%

commit v1 on v0

v1 whole, which is shorter than its diff:
```python
import functools
import math

import jax
import jax.numpy as jnp
from jax import lax
from jax.experimental import pallas as pl
from jax.experimental.pallas import tpu as pltpu
from jax.sharding import PartitionSpec as P

NVX = 24
HALF = NVX // 2
CHUNK = HALF * NVX
STEPS = 2
LIMIT = 4.0
COURANT = 0.1
SPACING = 2.0 * LIMIT / (NVX - 1)
WEIGHT = SPACING**3 / (2.0 * math.pi) ** 1.5
MESH = pl.DeviceIdType.MESH
LANES = 128
UNROLL = 2


def median0(p, r):
    return jnp.maximum(jnp.minimum(p, r), jnp.minimum(jnp.maximum(p, r), 0.0))


def sweep_rows(g, c, ck):
    d = [g[k + 1] - g[k] for k in range(6)]
    t = [ck * median0(d[k - 1], d[k]) for k in range(1, 6)]
    return [(g[k] - c * d[k - 1]) - (t[k - 1] - t[k - 2]) for k in range(2, 6)]


def sweep_lanes(f, c, ck, up_shift, down_shift, up_edge, down_edge):
    after = jnp.where(down_edge, 0.0, pltpu.roll(f, down_shift, 1))
    d = after - f
    before = jnp.where(up_edge, f, pltpu.roll(d, up_shift, 1))
    flux = c * f + ck * median0(before, d)
    return f - (flux - jnp.where(up_edge, 0.0, pltpu.roll(flux, up_shift, 1)))


def cell_parameters(total, kind):
    m = [total[k : k + 1] * WEIGHT for k in range(13)]
    rho = m[0]
    u = [m[1] / rho, m[2] / rho, m[3] / rho]
    energy = m[4] + m[5] + m[6]
    uu = u[0] * u[0] + u[1] * u[1] + u[2] * u[2]
    level = (energy / rho - uu) / 3.0
    um = u[0] * m[1] + u[1] * m[2] + u[2] * m[3]
    tail = energy - 2.0 * um + uu * rho
    second = [(4, 7, 8), (7, 5, 9), (8, 9, 6)]
    heat = []
    for i in range(3):
        mixed = sum(u[j] * m[second[i][j]] for j in range(3))
        heat.append(0.5 * (m[10 + i] - 2.0 * mixed + uu * m[1 + i] - u[i] * tail))
    inverse = 1.0 / level
    rate = 0.25 * rho * jnp.exp((1.0 - 0.81) * jnp.log(level))
    factor = rate * rho * inverse * lax.rsqrt(level)
    coupling = (1.0 - 2.0 / 3.0) / (5.0 * rho * level * level)
    gas = kind == 0
    wall = kind == 1
    zero = jnp.zeros_like(rho)
    rows = [
        jnp.where(gas, u[0], jnp.where(wall, 0.0, 0.5)),
        jnp.where(gas, u[1], 0.0),
        jnp.where(gas, u[2], 0.0),
        jnp.where(gas, inverse, 1.0),
        jnp.where(gas, coupling * heat[0], 0.0),
        jnp.where(gas, coupling * heat[1], 0.0),
        jnp.where(gas, coupling * heat[2], 0.0),
        jnp.where(gas, factor, jnp.where(wall, rho, 1.0)),
        jnp.where(gas, 1.0 - rate, 0.0),
        level,
    ]
    return jnp.concatenate(rows + [zero] * 6, axis=0)


def kernel(
    nv, ns, nchunk,
    x_ref, kind_ref, out_ref, level_ref,
    stage, first, second, third, halo1, halo2,
    acc, mom, gathered, par, near, tab_e, tab_o, tab_b,
    in_sem, out_sem, hs_down, hr_up, hs_up, hr_down,
    rs_send, rs_recv, ag_send, ag_recv, np_send, np_recv,
):
    me_v = lax.axis_index("vel")
    me_s = lax.axis_index("space")
    group = nv // 4
    positive = jnp.where(me_v >= nv // 2, 1, 0)
    sign = 2 * positive - 1
    down = me_s + sign
    up = me_s - sign
    has_down = jnp.logical_and(down >= 0, down < ns)
    has_up = jnp.logical_and(up >= 0, up < ns)
    down = jnp.clip(down, 0, ns - 1)
    up = jnp.clip(up, 0, ns - 1)
    halos = (halo1, halo2)

    def row_of(j):
        return j * sign + 3 * (1 - positive)

    def load_in(i):
        rows = pl.ds(pl.multiple_of(i * 4 * CHUNK, 4 * CHUNK), 4 * CHUNK)
        return pltpu.make_async_copy(x_ref.at[rows], stage.at[rows], in_sem.at[i])

    def store_out(i):
        rows = pl.ds(pl.multiple_of(i * 4 * CHUNK, 4 * CHUNK), 4 * CHUNK)
        return pltpu.make_async_copy(stage.at[rows], out_ref.at[rows], out_sem.at[i])

    def halo_down(step, src, i):
        rows = pl.ds(pl.multiple_of(i * CHUNK, CHUNK), CHUNK)
        return pltpu.make_async_remote_copy(
            src_ref=src.at[pl.ds(2, 2), rows], dst_ref=halos[step].at[pl.ds(0, 2), rows],
            send_sem=hs_down.at[step, i], recv_sem=hr_up.at[step, i],
            device_id={"space": down}, device_id_type=MESH)

    def halo_up(step, src, i):
        rows = pl.ds(pl.multiple_of(i * CHUNK, CHUNK), CHUNK)
        return pltpu.make_async_remote_copy(
            src_ref=src.at[pl.ds(0, 1), rows], dst_ref=halos[step].at[pl.ds(2, 1), rows],
            send_sem=hs_up.at[step, i], recv_sem=hr_down.at[step, i],
            device_id={"space": up}, device_id_type=MESH)

    def send_halo(step, src, i):
        @pl.when(has_down)
        def _():
            halo_down(step, src, i).start()

        @pl.when(has_up)
        def _():
            halo_up(step, src, i).start()

    def wait_halo(step, src, i):
        @pl.when(has_up)
        def _():
            halo_down(step, src, i).wait_recv()

        @pl.when(has_down)
        def _():
            halo_up(step, src, i).wait_recv()

    def wait_sent(step, src, i):
        @pl.when(has_down)
        def _():
            halo_down(step, src, i).wait_send()

        @pl.when(has_up)
        def _():
            halo_up(step, src, i).wait_send()

    pl.loop(0, nchunk)(lambda i: load_in(i).start())

    barrier = pltpu.get_barrier_semaphore()
    for k in range(1, nv):
        pl.semaphore_signal(barrier, inc=1, device_id={"vel": lax.rem(me_v + k, nv)}, device_id_type=MESH)

    @pl.when(has_down)
    def _():
        pl.semaphore_signal(barrier, inc=1, device_id={"space": down}, device_id_type=MESH)

    @pl.when(has_up)
    def _():
        pl.semaphore_signal(barrier, inc=1, device_id={"space": up}, device_id_type=MESH)

    @pl.when(jnp.logical_not(has_up))
    def _():
        def fill(i):
            for halo in halos:
                for n in range(2):
                    halo[n, pl.ds(pl.multiple_of(i * 32, 32), 32), :] = jnp.zeros((32, LANES), jnp.float32)
        pl.loop(0, nchunk * CHUNK // 32)(fill)
        near[0] = jnp.zeros((16, LANES), jnp.float32)
        near[1] = jnp.zeros((16, LANES), jnp.float32)

    @pl.when(jnp.logical_not(has_down))
    def _():
        def fill(i):
            for halo in halos:
                halo[2, pl.ds(pl.multiple_of(i * 32, 32), 32), :] = jnp.zeros((32, LANES), jnp.float32)
        pl.loop(0, nchunk * CHUNK // 32)(fill)
        near[2] = jnp.zeros((16, LANES), jnp.float32)

    pl.semaphore_wait(barrier, nv - 1 + jnp.where(has_down, 1, 0) + jnp.where(has_up, 1, 0))

    def spread(i):
        load_in(i).wait()

        def tile(n):
            for m in range(4):
                v = pl.multiple_of(i * CHUNK + n * 32, 32) + 8 * m
                for j in range(4):
                    first[j, pl.ds(v, 8), :] = stage[pl.ds(v * 4 + row_of(j), 8, stride=4), :]
        pl.loop(0, CHUNK // 32)(tile)
        send_halo(0, first, i)
    pl.loop(0, nchunk)(spread)

    sub = lax.broadcasted_iota(jnp.int32, (8, LANES), 0)
    lane = lax.broadcasted_iota(jnp.int32, (8, LANES), 1)

    def clear():
        for k in range(13):
            for j in range(4):
                acc[k, j] = jnp.zeros((8, LANES), jnp.float32)

    def speed(index):
        return -LIMIT + SPACING * index.astype(jnp.float32)

    def move(i, src, halo, dst, collided):
        chunk = me_v * nchunk + i
        half = lax.rem(chunk, 2)
        x1 = speed(chunk // 2)
        cx = COURANT * jnp.abs(x1)
        ckx = cx * 0.5 * (1.0 - cx)
        up_shift = jnp.where(half == 1, 1, LANES - 1)
        down_shift = LANES - up_shift
        up_lane = jnp.where(half == 1, 0, LANES - 1)
        up_edge = lane == up_lane
        down_edge = lane == LANES - 1 - up_lane
        base = i * CHUNK
        for e in range(NVX // 8):
            def one(b, sums):
                v = pl.ds(pl.multiple_of(base + b * NVX + 8 * e, 8), 8)
                x2 = speed(half * HALF + b)
                cy = COURANT * jnp.abs(x2)
                cky = cy * 0.5 * (1.0 - cy)
                g = [halo[0, v, :], halo[1, v, :]] + [src[j, v, :] for j in range(4)] + [halo[2, v, :]]
                if collided:
                    g = [collide(g[n], n, b, e) for n in range(7)]
                g = sweep_rows(g, cx, ckx)
                new = []
                for j in range(4):
                    o = sweep_lanes(g[j], cy, cky, up_shift, down_shift, up_edge, down_edge)
                    dst[j, v, :] = o
                    s0, s1, s2, s3 = sums[4 * j : 4 * j + 4]
                    o1 = x2 * o
                    o2 = x2 * o1
                    new += [s0 + o, s1 + o1, s2 + o2, s3 + x2 * o2]
                return tuple(new)

            def several(n, sums):
                for m in range(UNROLL):
                    sums = one(n * UNROLL + m, sums)
                return sums

            sums = lax.fori_loop(0, HALF // UNROLL, several, (jnp.zeros((8, LANES), jnp.float32),) * 16)
            x3 = speed(sub + 8 * e)
            for j in range(4):
                s0, s1, s2, s3 = sums[4 * j : 4 * j + 4]
                t1 = x1 * s0
                t3 = x3 * s0
                t11 = x1 * t1
                t33 = x3 * t3
                whole = t11 + s2 + t33
                terms = [s0, t1, s1, t3, t11, s2, t33, x1 * s1, x1 * t3, x3 * s1,
                         x1 * whole, (x1 * x1 + x3 * x3) * s1 + s3, x3 * whole]
                for k in range(13):
                    acc[k, j] = acc[k, j] + terms[k]

    def reduce(step):
        for j in range(4):
            rows = [jnp.sum(acc[k, j], axis=0, keepdims=True) for k in range(13)]
            mom[step, row_of(j)] = jnp.concatenate(rows + [jnp.zeros((3, LANES), jnp.float32)], axis=0)
        mine = me_v // group

        def part(k):
            to = lax.rem(me_v + k, nv)
            return pltpu.make_async_remote_copy(
                src_ref=mom.at[step, to // group], dst_ref=gathered.at[step, me_v],
                send_sem=rs_send.at[step, k], recv_sem=rs_recv.at[step, me_v],
                device_id={"vel": to}, device_id_type=MESH)

        def part_in(k):
            frm = lax.rem(me_v + k, nv)
            return pltpu.make_async_remote_copy(
                src_ref=mom.at[step, 0], dst_ref=gathered.at[step, frm],
                send_sem=rs_send.at[step, k], recv_sem=rs_recv.at[step, frm],
                device_id={"vel": frm}, device_id_type=MESH)

        for k in range(1, nv):
            part(k).start()
        gathered[step, me_v] = mom[step, mine]
        for k in range(1, nv):
            part_in(k).wait_recv()
        total = gathered[step, 0]
        for n in range(1, nv):
            total = total + gathered[step, n]
        par[step, mine] = cell_parameters(total, kind_ref[pl.ds(mine, 1), :])

        def share(k):
            to = lax.rem(mine + k, 4) * group + lax.rem(me_v, group)
            return pltpu.make_async_remote_copy(
                src_ref=par.at[step, mine], dst_ref=par.at[step, mine],
                send_sem=ag_send.at[step, k], recv_sem=ag_recv.at[step, mine],
                device_id={"vel": to}, device_id_type=MESH)

        def share_in(k):
            row = lax.rem(mine + k, 4)
            return pltpu.make_async_remote_copy(
                src_ref=par.at[step, mine], dst_ref=par.at[step, row],
                send_sem=ag_send.at[step, k], recv_sem=ag_recv.at[step, row],
                device_id={"vel": row * group + lax.rem(me_v, group)}, device_id_type=MESH)

        for k in range(1, 4):
            share(k).start()
        for k in range(1, 4):
            share_in(k).wait_recv()
        for k in range(1, nv):
            part(k).wait_send()
        for k in range(1, 4):
            share(k).wait_send()

    def near_copy(n):
        j, to = ((2, down), (3, down), (0, up))[n]
        return pltpu.make_async_remote_copy(
            src_ref=par.at[0, row_of(j)], dst_ref=near.at[n],
            send_sem=np_send.at[n], recv_sem=np_recv.at[n],
            device_id={"space": to}, device_id_type=MESH)

    def parameters(step, n):
        if n in (0, 1):
            return near[n]
        if n == 6:
            return near[2]
        return par[step, row_of(n - 2)]

    def build_e(step, rows):
        x3 = speed(lax.broadcasted_iota(jnp.int32, (NVX, LANES), 0))
        for n in rows:
            p = parameters(step, n)
            c3 = x3 - p[2:3]
            quad = c3 * c3 * p[3:4]
            tab_e[0, n] = quad
            tab_e[1, n] = p[6:7] * c3
            tab_e[2, n] = jnp.exp(-0.5 * quad)
            tab_o[n] = jnp.broadcast_to(p[8:9], (8, LANES))

    def build_b(step, i, rows):
        chunk = me_v * nchunk + i
        x1 = speed(chunk // 2)
        x2 = speed(lax.rem(chunk, 2) * HALF + lax.broadcasted_iota(jnp.int32, (16, LANES), 0))
        for n in rows:
            p = parameters(step, n)
            c1 = x1 - p[0:1]
            c2 = x2 - p[1:2]
            quad = (c1 * c1 + c2 * c2) * p[3:4]
            tab_b[0, n] = quad - 5.0
            tab_b[1, n] = p[4:5] * c1 + p[5:6] * c2
            tab_b[2, n] = p[7:8] * jnp.exp(-0.5 * quad)

    def collide(f, n, b, e):
        es = pl.ds(8 * e, 8)
        bs = pl.ds(b, 1)
        quad = tab_b[0, n, bs, :] + tab_e[0, n, es, :]
        flow = tab_b[1, n, bs, :] + tab_e[1, n, es, :]
        gauss = tab_b[2, n, bs, :] * tab_e[2, n, es, :]
        return tab_o[n] * f + gauss * (1.0 + flow * quad)

    clear()

    def step_one(i):
        wait_halo(0, first, i)
        move(i, first, halo1, second, False)
        send_halo(1, second, i)
    pl.loop(0, nchunk)(step_one)
    reduce(0)

    @pl.when(has_down)
    def _():
        near_copy(0).start()
        near_copy(1).start()

    @pl.when(has_up)
    def _():
        near_copy(2).start()
    clear()

    @pl.when(has_up)
    def _():
        near_copy(0).wait_recv()
        near_copy(1).wait_recv()

    @pl.when(has_down)
    def _():
        near_copy(2).wait_recv()

    build_e(0, range(7))

    def step_two(i):
        build_b(0, i, range(7))
        wait_halo(1, second, i)
        move(i, second, halo2, third, True)
    pl.loop(0, nchunk)(step_two)
    reduce(1)

    own = range(2, 6)
    build_e(1, own)

    def finish(i):
        build_b(1, i, own)
        for e in range(NVX // 8):
            def one(n):
                for m in range(UNROLL):
                    b = n * UNROLL + m
                    v = pl.multiple_of(i * CHUNK + b * NVX + 8 * e, 8)
                    for j in range(4):
                        stage[pl.ds(v * 4 + row_of(j), 8, stride=4), :] = collide(
                            third[j, pl.ds(v, 8), :], j + 2, b, e)
            pl.loop(0, HALF // UNROLL)(one)
        store_out(i).start()
    pl.loop(0, nchunk)(finish)

    for r in range(4):
        level_ref[r : r + 1, :] = par[1, r, 9:10, :]

    def drain(i):
        wait_sent(0, first, i)
        wait_sent(1, second, i)
        store_out(i).wait()
    pl.loop(0, nchunk)(drain)

    @pl.when(has_down)
    def _():
        near_copy(0).wait_send()
        near_copy(1).wait_send()

    @pl.when(has_up)
    def _():
        near_copy(2).wait_send()


def per_device(nv, ns, initial, site_kind):
    amount, rows, lanes = initial.shape
    assert rows == 4 and lanes == LANES and amount % CHUNK == 0
    assert nv % 4 == 0 and (NVX * NVX * HALF) % amount == 0
    nchunk = amount // CHUNK
    f32 = jnp.float32
    dma = pltpu.SemaphoreType.DMA
    out, level = pl.pallas_call(
        functools.partial(kernel, nv, ns, nchunk),
        out_shape=(
            jax.ShapeDtypeStruct((amount * 4, LANES), f32),
            jax.ShapeDtypeStruct((4, LANES), f32),
        ),
        in_specs=[pl.BlockSpec(memory_space=pl.ANY), pl.BlockSpec(memory_space=pltpu.VMEM)],
        out_specs=(pl.BlockSpec(memory_space=pl.ANY), pl.BlockSpec(memory_space=pltpu.VMEM)),
        scratch_shapes=[
            pltpu.VMEM((amount * 4, LANES), f32),
            pltpu.VMEM((4, amount, LANES), f32),
            pltpu.VMEM((4, amount, LANES), f32),
            pltpu.VMEM((4, amount, LANES), f32),
            pltpu.VMEM((3, amount, LANES), f32),
            pltpu.VMEM((3, amount, LANES), f32),
            pltpu.VMEM((13, 4, 8, LANES), f32),
            pltpu.VMEM((2, 4, 16, LANES), f32),
            pltpu.VMEM((2, nv, 16, LANES), f32),
            pltpu.VMEM((2, 4, 16, LANES), f32),
            pltpu.VMEM((3, 16, LANES), f32),
            pltpu.VMEM((3, 7, NVX, LANES), f32),
            pltpu.VMEM((7, 8, LANES), f32),
            pltpu.VMEM((3, 7, 16, LANES), f32),
            dma((nchunk,)), dma((nchunk,)),
            dma((2, nchunk)), dma((2, nchunk)), dma((2, nchunk)), dma((2, nchunk)),
            dma((2, nv)), dma((2, nv)), dma((2, 4)), dma((2, 4)), dma((3,)), dma((3,)),
        ],
        compiler_params=pltpu.CompilerParams(
            collective_id=0, has_side_effects=True, vmem_limit_bytes=40 * 1024 * 1024
        ),
    )(initial.reshape(amount * 4, LANES), site_kind)
    return out.reshape(amount, 4, LANES), level


def solution(mesh):
    return jax.shard_map(
        functools.partial(per_device, mesh.shape["vel"], mesh.shape["space"]),
        mesh=mesh,
        in_specs=(P("vel", "space", None), P("space", None)),
        out_specs=(P("vel", "space", None), P("space", None)),
        check_vma=False,
    )
```

time: 283 us -> 92.7 us (0.33)
  the two profiles are of different devices: /device:TPU:6 before, /device:TPU:0 now
where the time goes in v1:
time: 92.7 us; the launch traced here: 92.5 us
  Pallas kernels  86.8 us (94%)
  local copies, waits for them, and re-layouts  5.05 us (5%)
    pallas_call x1, Pallas kernels, per_device(): pl.pallas_call(functools.partial(kernel, nv, ns, nchunk), out_shape=(jax....  86.8 us
    unnamed x6, local copies, waits for them, and re-layouts  5.05 us

profile of v1, /device:TPU:0, one launch (start us, length us, event | category | flops | bytes accessed | tf_op | source)
XLA Modules:
  0.0 92.5 jit_solution(1648897500559703825)
XLA Ops:
  0.6 0.0 copy-start
  0.6 2.0 %copy-done = f32[1728,4,128]{2,1,0:T(4,128)S(1)} copy-done((f32[1728,4,128]{2,1,0:T(4,128)S(1)}, f32[1728,4,128]{2,1,0:T(4,128)}, u32[]{:S(2)}) %copy-start) | copy-done | bytes 3538968
  2.6 0.0 copy-start.1
  2.6 0.7 copy-done.1
  3.3 86.8 %shard_map.41 = (f32[6912,128]{1,0:T(8,128)S(1)}, f32[4,128]{1,0:T(4,128)S(1)}) custom-call(f32[6912,128]{1,0:T(8,128)S(1)} %bitcast.3, s32[4,128]{1,0:T(4,128)S(1)} %copy-done.1), custom_call_target="tpu_custom_call" | custom-call | tf_op jit(solution)/shard_map/pallas_call | solution.py:438
  90.1 1.8 %copy.6 = f32[1728,4,128]{2,1,0:T(4,128)} copy(f32[1728,4,128]{2,1,0:T(4,128)S(1)} %bitcast.2) | data formatting | bytes 7077888
  91.9 0.6 copy.7
Async XLA Ops:
  0.6 2.0 %copy-start = (f32[1728,4,128]{2,1,0:T(4,128)S(1)}, f32[1728,4,128]{2,1,0:T(4,128)}, u32[]{:S(2)}) copy-start(f32[1728,4,128]{2,1,0:T(4,128)} %param.2) | copy-start | bytes 10616836
  2.6 0.7 copy-start.1

commit v2 on v1

--- a/solution.py
+++ b/solution.py
@@ -18,7 +18,7 @@
 WEIGHT = SPACING**3 / (2.0 * math.pi) ** 1.5
 MESH = pl.DeviceIdType.MESH
 LANES = 128
-UNROLL = 2
+UNROLL = 6
 
 
 def median0(p, r):
@@ -95,6 +95,7 @@
     down = jnp.clip(down, 0, ns - 1)
     up = jnp.clip(up, 0, ns - 1)
     halos = (halo1, halo2)
+    early = nchunk // 2
 
     def row_of(j):
         return j * sign + 3 * (1 - positive)
@@ -360,7 +361,10 @@
     def step_one(i):
         wait_halo(0, first, i)
         move(i, first, halo1, second, False)
-        send_halo(1, second, i)
+
+        @pl.when(i < early)
+        def _():
+            send_halo(1, second, i)
     pl.loop(0, nchunk)(step_one)
     reduce(0)
 
@@ -372,6 +376,7 @@
     @pl.when(has_up)
     def _():
         near_copy(2).start()
+    pl.loop(early, nchunk)(lambda i: send_halo(1, second, i))
     clear()
 
     @pl.when(has_up)

time: 92.7 us -> 67.3 us (0.73)
  Pallas kernels: 86.8 us -> 61.4 us
    pallas_call x1, Pallas kernels: 86.8 us -> 61.4 us  [per_device(): pl.pallas_call(functools.partial(kernel, nv, ns, nchunk), out_shape=(jax....]
where the time goes in v2:
time: 67.3 us; the launch traced here: 67.1 us
  Pallas kernels  61.4 us (91%)
  local copies, waits for them, and re-layouts  5.05 us (8%)
    pallas_call x1, Pallas kernels, per_device(): pl.pallas_call(functools.partial(kernel, nv, ns, nchunk), out_shape=(jax....  61.4 us
    unnamed x6, local copies, waits for them, and re-layouts  5.05 us

profile of v2, /device:TPU:0, one launch (start us, length us, event | category | flops | bytes accessed | tf_op | source)
XLA Modules:
  0.0 67.1 jit_solution(8810303322723167090)
XLA Ops:
  0.6 0.0 copy-start
  0.6 2.0 %copy-done = f32[1728,4,128]{2,1,0:T(4,128)S(1)} copy-done((f32[1728,4,128]{2,1,0:T(4,128)S(1)}, f32[1728,4,128]{2,1,0:T(4,128)}, u32[]{:S(2)}) %copy-start) | copy-done | bytes 3538968
  2.6 0.0 copy-start.1
  2.6 0.7 %copy-done.1 = s32[4,128]{1,0:T(4,128)S(1)} copy-done((s32[4,128]{1,0:T(4,128)S(1)}, s32[4,128]{1,0:T(4,128)}, u32[]{:S(2)}) %copy-start.1) | copy-done | bytes 2072
  3.3 61.4 %shard_map.41 = (f32[6912,128]{1,0:T(8,128)S(1)}, f32[4,128]{1,0:T(4,128)S(1)}) custom-call(f32[6912,128]{1,0:T(8,128)S(1)} %bitcast.3, s32[4,128]{1,0:T(4,128)S(1)} %copy-done.1), custom_call_target="tpu_custom_call" | custom-call | tf_op jit(solution)/shard_map/pallas_call | solution.py:443
  64.7 1.8 %copy.6 = f32[1728,4,128]{2,1,0:T(4,128)} copy(f32[1728,4,128]{2,1,0:T(4,128)S(1)} %bitcast.2) | data formatting | bytes 7077888
  66.5 0.6 copy.7
Async XLA Ops:
  0.6 2.0 %copy-start = (f32[1728,4,128]{2,1,0:T(4,128)S(1)}, f32[1728,4,128]{2,1,0:T(4,128)}, u32[]{:S(2)}) copy-start(f32[1728,4,128]{2,1,0:T(4,128)} %param.2) | copy-start | bytes 10616836
  2.6 0.7 %copy-start.1 = (s32[4,128]{1,0:T(4,128)S(1)}, s32[4,128]{1,0:T(4,128)}, u32[]{:S(2)}) copy-start(s32[4,128]{1,0:T(4,128)} %kind_ref.1) | copy-start | bytes 6148

commit v3 on v2

--- a/solution.py
+++ b/solution.py
@@ -80,7 +80,7 @@
     x_ref, kind_ref, out_ref, level_ref,
     stage, first, second, third, halo1, halo2,
     acc, mom, gathered, par, near, tab_e, tab_o, tab_b,
-    in_sem, out_sem, hs_down, hr_up, hs_up, hr_down,
+    in_sem, hs_down, hr_up, hs_up, hr_down,
     rs_send, rs_recv, ag_send, ag_recv, np_send, np_recv,
 ):
     me_v = lax.axis_index("vel")
@@ -103,10 +103,6 @@
     def load_in(i):
         rows = pl.ds(pl.multiple_of(i * 4 * CHUNK, 4 * CHUNK), 4 * CHUNK)
         return pltpu.make_async_copy(x_ref.at[rows], stage.at[rows], in_sem.at[i])
-
-    def store_out(i):
-        rows = pl.ds(pl.multiple_of(i * 4 * CHUNK, 4 * CHUNK), 4 * CHUNK)
-        return pltpu.make_async_copy(stage.at[rows], out_ref.at[rows], out_sem.at[i])
 
     def halo_down(step, src, i):
         rows = pl.ds(pl.multiple_of(i * CHUNK, CHUNK), CHUNK)
@@ -408,10 +404,9 @@
                     b = n * UNROLL + m
                     v = pl.multiple_of(i * CHUNK + b * NVX + 8 * e, 8)
                     for j in range(4):
-                        stage[pl.ds(v * 4 + row_of(j), 8, stride=4), :] = collide(
+                        out_ref[pl.ds(v * 4 + row_of(j), 8, stride=4), :] = collide(
                             third[j, pl.ds(v, 8), :], j + 2, b, e)
             pl.loop(0, HALF // UNROLL)(one)
-        store_out(i).start()
     pl.loop(0, nchunk)(finish)
 
     for r in range(4):
@@ -420,7 +415,6 @@
     def drain(i):
         wait_sent(0, first, i)
         wait_sent(1, second, i)
-        store_out(i).wait()
     pl.loop(0, nchunk)(drain)
 
     @pl.when(has_down)
@@ -447,7 +441,7 @@
             jax.ShapeDtypeStruct((4, LANES), f32),
         ),
         in_specs=[pl.BlockSpec(memory_space=pl.ANY), pl.BlockSpec(memory_space=pltpu.VMEM)],
-        out_specs=(pl.BlockSpec(memory_space=pl.ANY), pl.BlockSpec(memory_space=pltpu.VMEM)),
+        out_specs=(pl.BlockSpec(memory_space=pltpu.VMEM), pl.BlockSpec(memory_space=pltpu.VMEM)),
         scratch_shapes=[
             pltpu.VMEM((amount * 4, LANES), f32),
             pltpu.VMEM((4, amount, LANES), f32),
@@ -463,12 +457,12 @@
             pltpu.VMEM((3, 7, NVX, LANES), f32),
             pltpu.VMEM((7, 8, LANES), f32),
             pltpu.VMEM((3, 7, 16, LANES), f32),
-            dma((nchunk,)), dma((nchunk,)),
+            dma((nchunk,)),
             dma((2, nchunk)), dma((2, nchunk)), dma((2, nchunk)), dma((2, nchunk)),
             dma((2, nv)), dma((2, nv)), dma((2, 4)), dma((2, 4)), dma((3,)), dma((3,)),
         ],
         compiler_params=pltpu.CompilerParams(
-            collective_id=0, has_side_effects=True, vmem_limit_bytes=40 * 1024 * 1024
+            collective_id=0, has_side_effects=True, vmem_limit_bytes=50 * 1024 * 1024
         ),
     )(initial.reshape(amount * 4, LANES), site_kind)
     return out.reshape(amount, 4, LANES), level

time: 67.3 us -> 63.7 us (0.947)
  local copies, waits for them, and re-layouts: 5.05 us -> 3.05 us
  Pallas kernels: 61.4 us -> 59.8 us
    unnamed x6 -> x4, local copies, waits for them, and re-layouts: 5.05 us -> 3.05 us
    pallas_call x1, Pallas kernels: 61.4 us -> 59.8 us  [per_device(): pl.pallas_call(functools.partial(kernel, nv, ns, nchunk), out_shape=(jax....]
where the time goes in v3:
time: 63.7 us; the launch traced here: 63.5 us
  Pallas kernels  59.8 us (94%)
  local copies, waits for them, and re-layouts  3.05 us (5%)
  between operations  0.65 us (1%)
    pallas_call x1, Pallas kernels, per_device(): pl.pallas_call(functools.partial(kernel, nv, ns, nchunk), out_shape=(jax....  59.8 us
    unnamed x4, local copies, waits for them, and re-layouts  3.05 us

profile of v3, /device:TPU:0, one launch (start us, length us, event | category | flops | bytes accessed | tf_op | source)
XLA Modules:
  0.0 63.5 jit_solution(14512122108769469182)
XLA Ops:
  0.6 0.0 copy-start
  0.6 0.7 %copy-done = s32[4,128]{1,0:T(4,128)S(1)} copy-done((s32[4,128]{1,0:T(4,128)S(1)}, s32[4,128]{1,0:T(4,128)}, u32[]{:S(2)}) %copy-start) | copy-done | bytes 2072
  1.3 59.8 %shard_map.41 = (f32[6912,128]{1,0:T(8,128)S(1)}, f32[4,128]{1,0:T(4,128)S(1)}) custom-call(f32[6912,128]{1,0:T(8,128)} %bitcast.3, s32[4,128]{1,0:T(4,128)S(1)} %copy-done), custom_call_target="tpu_custom_call" | custom-call | tf_op jit(solution)/shard_map/pallas_call | solution.py:437
  61.1 1.8 %copy.6 = f32[1728,4,128]{2,1,0:T(4,128)} copy(f32[1728,4,128]{2,1,0:T(4,128)S(1)} %bitcast.2) | data formatting | bytes 7077888
  62.9 0.6 copy.7
Async XLA Ops:
  0.6 0.7 %copy-start = (s32[4,128]{1,0:T(4,128)S(1)}, s32[4,128]{1,0:T(4,128)}, u32[]{:S(2)}) copy-start(s32[4,128]{1,0:T(4,128)} %kind_ref.1) | copy-start | bytes 6148
